TPU v7x, 256 devices: a whole 4x4x8 slice. The times are simulated.
256 devices in a mesh: dp: 8 (over z), tensor: 32 (over x, y, core).
Axes of the slice: x: 4, y: 4, z: 8, core: 2. Of those that a mesh axis runs over, the one named last changes fastest.
Arguments:
- hidden: bfloat16 [256, 16384], P('dp'), may hold values from -6 to 6
- gain: float32 [16384], replicated, may hold values from 0.1 to 1.9
- w_qkv: bfloat16 [16384, 24576], P('dp', 'tensor'), as said below
- cache: bfloat16 [256, 32, 256, 256], P('dp', 'tensor'), as said below
- lengths: int32 [256], P('dp'), may hold values from 32 to 256, as said below
- w_out: bfloat16 [16384, 16384], P('tensor', 'dp'), may hold values from -0.25 to 0.25
Outputs:
- output: bfloat16 [256, 16384], P('dp')
Inputs may be any that keep to these rules, and one draw needn't show every extreme that they name: `lengths`: in every draw some row has exactly 256 cached positions. `cache`: head group s holds the keys and values of key-value head s * 8 // 32. `w_qkv`: the key and value columns of head group s are those of key-value head s * 8 // 32.
All inputs are finite; a program needn't handle non-finite values.
Results may differ from a plain program's by a relative error of at most 0.022.
Values may be sent and summed in bfloat16 or wider, within the bound.
A program may use at most 128 MiB of HBM per device.

v0:
```python
import jax
import jax.numpy as jnp
from jax import lax
from jax.sharding import PartitionSpec as P

rope_base = 500000.0


def rotate(values, angles):
    half = values.shape[-1] // 2
    first = values[..., :half]
    second = values[..., half:]
    cosine = jnp.cos(angles)
    sine = jnp.sin(angles)
    return jnp.concatenate(
        [first * cosine - second * sine, second * cosine + first * sine], axis=-1
    )


def attend(projected, block, lengths, per_slot, head_size):
    rows = projected.shape[0]
    queries = projected[:, : per_slot * head_size].reshape(rows, per_slot, head_size)
    new_key = projected[:, per_slot * head_size : per_slot * head_size + head_size]
    new_value = projected[:, per_slot * head_size + head_size :]
    half = head_size // 2
    frequency = rope_base ** (-jnp.arange(half, dtype=jnp.float32) * 2.0 / head_size)
    angles = lengths.astype(jnp.float32)[:, None] * frequency[None, :]
    queries = rotate(queries, angles[:, None, :]).astype(jnp.bfloat16)
    new_key = rotate(new_key, angles).astype(jnp.bfloat16)
    new_value = new_value.astype(jnp.bfloat16)
    keys = block[..., :head_size]
    values = block[..., head_size:]
    scale = 1.0 / head_size**0.5
    scores = jnp.einsum("rhd,rcd->rhc", queries, keys, preferred_element_type=jnp.float32) * scale
    own = jnp.einsum("rhd,rd->rh", queries, new_key, preferred_element_type=jnp.float32) * scale
    valid = jnp.arange(block.shape[1])[None, :] < lengths[:, None]
    scores = jnp.where(valid[:, None, :], scores, -jnp.inf)
    largest = jnp.maximum(jnp.max(scores, axis=-1), own)
    weights = jnp.exp(scores - largest[..., None])
    own_weight = jnp.exp(own - largest)
    total = jnp.sum(weights, axis=-1) + own_weight
    probs = (weights / total[..., None]).astype(jnp.bfloat16)
    own_prob = (own_weight / total).astype(jnp.bfloat16)
    mixed = jnp.einsum("rhc,rcd->rhd", probs, values, preferred_element_type=jnp.float32)
    mixed = (
        mixed + own_prob.astype(jnp.float32)[..., None] * new_value.astype(jnp.float32)[:, None, :]
    )
    return mixed.astype(jnp.bfloat16).reshape(rows, per_slot * head_size)


def body(hidden, gain, w_qkv, cache, lengths, w_out):
    head_size = cache.shape[-1] // 2
    per_slot = w_out.shape[0] // head_size
    wide = hidden.astype(jnp.float32)
    square_mean = jnp.mean(wide * wide, axis=-1, keepdims=True)
    normed = (wide * lax.rsqrt(square_mean + 1e-05) * gain).astype(jnp.bfloat16)
    columns = lax.all_to_all(normed, "dp", split_axis=1, concat_axis=0, tiled=True)
    projected = lax.psum_scatter(
        jnp.dot(columns, w_qkv, preferred_element_type=jnp.float32),
        "dp",
        scatter_dimension=0,
        tiled=True,
    )
    attended = attend(projected, cache[:, 0], lengths, per_slot, head_size)
    partial_all = jnp.dot(
        lax.all_gather(attended, "dp", axis=0, tiled=True),
        w_out,
        preferred_element_type=jnp.float32,
    )
    partial_value = lax.all_to_all(
        partial_all.astype(jnp.bfloat16), "dp", split_axis=0, concat_axis=1, tiled=True
    ).astype(partial_all.dtype)
    summed = lax.psum(partial_value.astype(jnp.bfloat16), "tensor").astype(jnp.float32)
    result = (wide + summed).astype(jnp.bfloat16)
    return result


def solution(mesh):
    return jax.shard_map(
        body,
        mesh=mesh,
        in_specs=(
            P("dp", None),
            P(),
            P("dp", "tensor"),
            P("dp", "tensor", None, None),
            P("dp"),
            P("tensor", "dp"),
        ),
        out_specs=P("dp", None),
        check_vma=False,
    )
```

profile of v0, /device:TPU:1, one launch (start us, length us, event | category | flops | bytes accessed | tf_op | source)
XLA Modules:
  0.0 262.9 jit_solution(17079373095130675746)
XLA Ops:
  6.5 0.0 copy-start
  6.5 0.0 reduce-scatter.2.cloned.1.call-start
  6.5 1.7 fusion
  8.2 1.5 fusion.2
  9.8 0.1 copy.22
  9.9 36.0 %all_to_all.38 = bf16[32,8,2048]{2,0,1:T(8,128)(2,1)S(1)} all-to-all(bf16[32,8,2048]{2,0,1:T(8,128)(2,1)S(1)} %bitcast.26), channel_id=1, replica_groups=mesh['dp'=8,'tensor'=32] {'dp'}, dimensions={1} | all-to-all | bytes 2097152 | tf_op jit(solution)/shard_map/all_to_all | solution.py:57
  45.9 0.0 copy-done
  45.9 0.0 copy-start.2
  45.9 1.9 fusion.29
  47.8 0.0 reduce-scatter.2.cloned.1.call-update
  47.8 0.0 all-reduce.2.cloned.1.call-start
  47.8 0.0 copy-done.2
  47.9 0.1 iota_compare_fusion
  47.9 31.6 %reduce-scatter.2.cloned.1.call-done = f32[32,768]{1,0:T(8,128)} async-done(((f32[256,768]{1,0:T(8,128)}), f32[32,768]{1,0:T(8,128)}) %reduce-scatter.2.cloned.1.call-update) | async-done | bytes 98320 | tf_op jit(solution)/shard_map/reduce_scatter | solution.py:58
  79.6 0.8 slice.36
  80.4 0.9 subtract_convert_fusion.1
  81.4 0.1 maximum_bitcast_fusion
  81.4 0.1 subtract_convert_fusion
  81.6 0.2 fusion.23
  81.8 2.4 fusion.28
  84.1 0.0 copy-start.1
  84.2 0.2 fusion.20
  84.4 0.8 fusion.26
  85.2 2.0 fusion.17
  87.3 18.9 %all_gather.3 = bf16[256,512]{1,0:T(8,128)(2,1)S(1)} all-gather(bf16[32,512]{1,0:T(8,128)(2,1)S(1)} %bitcast.30), channel_id=1, replica_groups=mesh['dp'=8,'tensor'=32] {'dp'}, dimensions={0}, use_global_device_ids=true | all-gather | bytes 294912 | tf_op jit(solution)/shard_map/all_gather | solution.py:66
  106.2 0.0 copy-done.1
  106.2 0.7 convolution_convert_fusion
  106.9 21.3 %all_to_all.39 = bf16[8,32,2048]{2,1,0:T(8,128)(2,1)S(1)} all-to-all(bf16[8,32,2048]{2,1,0:T(8,128)(2,1)S(1)} %bitcast.27), channel_id=1, replica_groups=mesh['dp'=8,'tensor'=32] {'dp'}, dimensions={0} | all-to-all | bytes 2097152 | tf_op jit(solution)/shard_map/all_to_all | solution.py:70
  128.2 1.0 copy.16
  129.2 0.0 all-reduce.2.cloned.1.call-update
  129.3 124.0 %all-reduce.2.cloned.1.call-done = bf16[32,16384]{1,0:T(8,128)(2,1)} async-done(((bf16[32,16384]{1,0:T(8,128)(2,1)}), bf16[32,16384]{1,0:T(8,128)(2,1)}) %all-reduce.2.cloned.1.call-update) | async-done | bytes 1048592 | tf_op jit(solution)/shard_map/psum | solution.py:73
  253.3 2.7 %fusion.3 = bf16[32,16384]{1,0:T(8,128)(2,1)} fusion(bf16[32,16384]{1,0:T(8,128)(2,1)} %param.6, bf16[32,16384]{1,0:T(8,128)(2,1)} %all-reduce.2.cloned.1.call-done), kind=kLoop, calls=%fused_computation.7 | loop fusion | flops 2097152 | bytes 3145728 | tf_op jit(solution)/shard_map/convert_element_type | solution.py:74
  (7 shorter events, 0.1 us)
Async XLA Ops:
  6.5 39.4 %copy-start = (bf16[2048,768]{1,0:T(8,128)(2,1)S(1)}, bf16[2048,768]{1,0:T(8,128)(2,1)}, u32[]{:S(2)}) copy-start(bf16[2048,768]{1,0:T(8,128)(2,1)} %param.8) | copy-start | bytes 9437188
  6.5 73.0 %reduce-scatter.2.cloned.1.call-start = ((), (), s32[]{:S(2)}) async-start(), calls=%async_computation.3 | async-start | bytes 884736 | tf_op jit(solution)/shard_map/reduce_scatter | solution.py:58
  45.9 1.9 copy-start.2
  47.8 205.5 %all-reduce.2.cloned.1.call-start = ((), (), s32[]{:S(2)}) async-start(), calls=%async_computation.4 | async-start | bytes 2097152 | tf_op jit(solution)/shard_map/psum | solution.py:73
  84.1 22.0 %copy-start.1 = (bf16[512,2048]{1,0:T(8,128)(2,1)S(1)}, bf16[512,2048]{1,0:T(8,128)(2,1)}, u32[]{:S(2)}) copy-start(bf16[512,2048]{1,0:T(8,128)(2,1)} %param.11) | copy-start | bytes 6291460
Sparse Core Ops, SparseCore 0:
  47.9 31.6 reduce-scatter.1
  129.4 123.8 all-reduce.1
where the time goes:
time: 263 us
  waiting for transfers between devices  156 us (59%)
  blocking collectives  76.2 us (29%)
  between operations  13.5 us (5%)
  other arithmetic  8.25 us (3%)
  matrix products  7.18 us (3%)
    psum x1, waiting for transfers between devices, body(): lax.psum(partial_value.astype(jnp.bfloat16), 'tensor').astype(jnp.float32)  124 us
    all_to_all x1, blocking collectives, body(): lax.all_to_all(normed, 'dp', split_axis=1, concat_axis=0, tiled=True)  36 us
    reduce_scatter x1, waiting for transfers between devices, body(): lax.psum_scatter(jnp.dot(columns, w_qkv, preferred_element_type=jnp.float...  31.6 us
    all_to_all x1, blocking collectives, body(): lax.all_to_all(partial_all.astype(jnp.bfloat16), 'dp', split_axis=0, conc...  21.3 us
    all_gather x1, blocking collectives, body(): lax.all_gather(attended, 'dp', axis=0, tiled=True)  18.9 us
  transfers between devices with their start and end apart: 2, of which 2 were waited for; matrix products, arithmetic and copies ran while one was open for 0% of the time, Pallas kernels for 0%

commit v1 on v0

v1 whole, which is shorter than its diff:
```python
import functools
import math

import jax
import jax.numpy as jnp
from jax import lax
from jax.experimental import pallas as pl
from jax.experimental.pallas import tpu as pltpu
from jax.sharding import PartitionSpec as P

DP = 8
CHIPS = 16
ROWS = 16
FEAT = 2048
HD = 128
QW = 512
NEAR = 5
ROPE_BASE = 500000.0
MESH = pl.DeviceIdType.MESH
F32 = jnp.float32
BF16 = jnp.bfloat16
FAR_ORDER = (6, 5, 7, 0, 4, 1, 3)
PLANE_ORDER = (10, 6, 14, 9, 11, 2, 8, 5, 7, 13, 15, 1, 3, 4, 12)


def kernel(
    hid,
    gain,
    wqkv,
    cache,
    lens,
    wout,
    out,
    x_s,
    far_in,
    far_out,
    gain_s,
    wq_s,
    wkv_s,
    wo_s,
    cache_s,
    hrow_s,
    pq_s,
    rq_s,
    pkv_s,
    rkv_s,
    nkv_s,
    at_s,
    acc_s,
    po_s,
    ro_s,
    ps_s,
    r5_s,
    fin_s,
    g_s,
    lsem,
    w_ss,
    w_rs,
    x_ss,
    x_rs,
    xp_ss,
    xp_rs,
    kv_ss,
    kv_rs,
    q_ss,
    q_rs,
    n_ss,
    n_rs,
    a_ss,
    a_rs,
    o_ss,
    o_rs,
    t_ss,
    t_rs,
    f_ss,
    f_rs,
    e_ss,
    e_rs,
    osem,
):
    d = lax.axis_index("dp")
    t = lax.axis_index("tensor")
    k = t % 2
    c = t // 2
    cx = c // 4
    cy = c % 4
    half = c % 2
    row0 = pl.multiple_of(k * ROWS, ROWS)
    sibling = (d, c * 2 + (1 - k))

    def block(g):
        return (d + g + 6) % DP

    def at_block(g):
        return (block(g), t)

    def chip(o):
        px = (cx + o // 4) % 4
        py = (cy + o % 4) % 4
        return px * 4 + py

    def back(o):
        px = (cx + 4 - o // 4) % 4
        py = (cy + 4 - o % 4) % 4
        return px * 4 + py

    def rdma(src, dst, ss, rs, dev):
        return pltpu.make_async_remote_copy(
            src_ref=src, dst_ref=dst, send_sem=ss, recv_sem=rs, device_id=dev, device_id_type=MESH
        )

    def lanes(index):
        return pl.ds(pl.multiple_of(index * 128, 128), 128)

    mine = pl.ds(pl.multiple_of(d * FEAT, FEAT), FEAT)
    l_x = pltpu.make_async_copy(hid.at[pl.ds(row0, ROWS), mine], x_s.at[2], lsem.at[0])
    l_gain = pltpu.make_async_copy(gain.at[:, mine], gain_s, lsem.at[1])
    l_h = pltpu.make_async_copy(hid.at[pl.ds(row0, ROWS), :], hrow_s, lsem.at[2])
    l_wq = pltpu.make_async_copy(wqkv.at[:, pl.ds(0, QW)], wq_s.at[k], lsem.at[3])
    l_wkv = pltpu.make_async_copy(
        wqkv.at[:, pl.ds(pl.multiple_of(QW + half * HD, HD), HD)], wkv_s, lsem.at[4]
    )
    l_cache = pltpu.make_async_copy(cache.at[pl.ds(row0, ROWS), 0], cache_s, lsem.at[5])
    l_wo = pltpu.make_async_copy(wout, wo_s.at[k], lsem.at[6])
    for copy in (l_gain, l_x, l_h, l_wkv, l_wq, l_cache, l_wo):
        copy.start()

    barrier = pltpu.get_barrier_semaphore()
    partners = [at_block(g) for g in FAR_ORDER]
    partners += [(d, chip(o) * 2 + k) for o in PLANE_ORDER]
    partners += [sibling]
    for dev in partners:
        pl.semaphore_signal(barrier, inc=1, device_id=dev, device_id_type=MESH)
    pl.semaphore_wait(barrier, len(partners))

    def x_copy(g):
        to = (d + 2 - g + DP) % DP
        rows = pl.ds(row0, ROWS)
        if g < NEAR:
            return rdma(
                hid.at[rows, pl.ds(pl.multiple_of(to * FEAT, FEAT), FEAT)],
                x_s.at[g],
                x_ss.at[g],
                x_rs.at[g],
                (to, t),
            )
        return rdma(
            hid.at[rows, pl.ds(pl.multiple_of(to * FEAT + c * 128, 128), 128)],
            far_in.at[g - NEAR],
            x_ss.at[g],
            x_rs.at[g],
            (to, t),
        )

    for g in FAR_ORDER:
        x_copy(g).start()
    w_copies = [
        rdma(wqkv.at[:, pl.ds(0, QW)], wq_s.at[k], w_ss.at[0], w_rs.at[0], sibling),
        rdma(wout, wo_s.at[k], w_ss.at[1], w_rs.at[1], sibling),
    ]
    for copy in w_copies:
        copy.start()

    l_h.wait()

    def square(i, total):
        cols = pl.ds(pl.multiple_of(i * 1024, 1024), 1024)
        part = hrow_s[:, cols].astype(F32)
        part = part * part
        for j in range(8):
            total = total + part[:, j * 128 : (j + 1) * 128]
        return total

    squares = lax.fori_loop(0, 16, square, jnp.zeros((ROWS, 128), F32))
    row_scale = lax.rsqrt(jnp.sum(squares, axis=1, keepdims=True) * (1.0 / (DP * FEAT)) + 1e-05)

    row_id = lax.broadcasted_iota(jnp.int32, (ROWS, HD), 0)
    lane_id = lax.broadcasted_iota(jnp.int32, (ROWS, HD), 1)
    length = jnp.zeros((ROWS, HD), jnp.int32)
    for b in range(ROWS):
        length = jnp.where(row_id == b, lens[k * ROWS + b], length)
    pair = jnp.where(lane_id < HD // 2, lane_id, lane_id - HD // 2).astype(F32)
    angle = length.astype(F32) * jnp.exp(pair * (-2.0 * math.log(ROPE_BASE) / HD))
    cosine = jnp.cos(angle)
    sine = jnp.sin(angle)
    sine = jnp.where(lane_id < HD // 2, -sine, sine)

    def rotate(v):
        return v * cosine + pltpu.roll(v, HD // 2, 1) * sine

    l_gain.wait()
    l_x.wait()

    def apply_gain(g):
        x_s[g] = (x_s[g].astype(F32) * gain_s[...]).astype(BF16)

    apply_gain(2)

    for g in (5, 7, 6):
        x_copy(g).wait_recv()
    here = gain_s[:, lanes(c)]
    tiles = (far_in[...].astype(F32) * here.reshape(1, 1, 128)).astype(BF16)
    far_out[...] = tiles
    x_s[pl.ds(NEAR, 3), :, lanes(c)] = tiles

    def xp_copy(o, src):
        return rdma(
            far_out,
            x_s.at[pl.ds(NEAR, 3), :, lanes(src)],
            xp_ss.at[o],
            xp_rs.at[o],
            (d, chip(o) * 2 + k),
        )

    for o in PLANE_ORDER:
        xp_copy(o, c).start()

    for g in (1, 3, 0, 4):
        x_copy(g).wait_recv()
        apply_gain(g)

    def kv_copy(g):
        return rdma(
            pkv_s.at[g], rkv_s.at[(12 - g) % DP], kv_ss.at[g], kv_rs.at[(12 - g) % DP], at_block(g)
        )

    def q_copy(s, g):
        return rdma(
            pq_s.at[s, g],
            rq_s.at[s, (12 - g) % DP],
            q_ss.at[s, g],
            q_rs.at[s, (12 - g) % DP],
            at_block(g),
        )

    def project(lo, n, order):
        lhs = x_s[pl.ds(lo, n)].reshape(n * ROWS, FEAT)
        got = jnp.dot(lhs, wkv_s[...], preferred_element_type=F32)
        pkv_s[pl.ds(lo, n)] = got.astype(BF16).reshape(n, ROWS, HD)
        for g in order:
            kv_copy(g).start()
        for s in range(2):
            for j in range(2):
                got = jnp.dot(
                    lhs, wq_s[s, :, j * 256 : (j + 1) * 256], preferred_element_type=F32
                )
                pq_s[s, pl.ds(lo, n), :, j * 256 : (j + 1) * 256] = got.astype(BF16).reshape(
                    n, ROWS, 256
                )
            for g in order:
                q_copy(s, g).start()

    l_wkv.wait()
    l_wq.wait()
    rdma(
        wqkv.at[:, pl.ds(0, QW)], wq_s.at[1 - k], w_ss.at[0], w_rs.at[0], sibling
    ).wait_recv()
    project(0, NEAR, (0, 4, 1, 3))
    for o in PLANE_ORDER:
        xp_copy(o, back(o)).wait_recv()
    project(NEAR, 3, (6, 5, 7))

    others = (3, 1, 4, 0, 7, 5, 6)
    total = pkv_s[2].astype(F32)
    for g in others:
        kv_copy((12 - g) % DP).wait_recv()
        total = total + rkv_s[g].astype(F32)
    total = total * row_scale
    nkv_s[half] = jnp.where(half == 0, rotate(total), total).astype(BF16)
    beside = cx * 4 + (cy // 2) * 2 + (1 - half)

    def n_copy(which):
        return rdma(
            nkv_s.at[which], nkv_s.at[which], n_ss.at[0], n_rs.at[0], (d, beside * 2 + k)
        )

    n_copy(half).start()

    l_cache.wait()
    wide_row = lax.broadcasted_iota(jnp.int32, (4 * ROWS, HD), 0) % ROWS
    wide_lane = lax.broadcasted_iota(jnp.int32, (256, 4 * ROWS), 1) % ROWS
    position = lax.broadcasted_iota(jnp.int32, (4 * ROWS, 256), 1)
    limit = jnp.concatenate([length[:, :1]] * 4, axis=0)
    scale = 1.0 / HD**0.5

    def a_copy(s, g):
        return rdma(
            at_s.at[s, :, 2],
            at_s.at[s, :, (12 - g) % DP],
            a_ss.at[s, g],
            a_rs.at[s, (12 - g) % DP],
            at_block(g),
        )

    for s in range(2):
        total = pq_s[s, 2].astype(F32)
        for g in others:
            q_copy(s, (12 - g) % DP).wait_recv()
            total = total + rq_s[s, g].astype(F32)
        total = total * row_scale
        queries = jnp.concatenate(
            [rotate(total[:, h * HD : (h + 1) * HD]) for h in range(4)], axis=0
        ).astype(BF16)
        turned = queries.astype(F32).T.astype(BF16)

        def score(i, scores):
            for j in range(4):
                b = i * 4 + j
                got = jnp.dot(cache_s[b, :, :HD], turned, preferred_element_type=F32)
                scores = jnp.where(wide_lane == b, got, scores)
            return scores

        scores = lax.fori_loop(0, 4, score, jnp.zeros((256, 4 * ROWS), F32))
        scores = jnp.where(position < limit, scores.T * scale, -jnp.inf)
        largest = jnp.max(scores, axis=1, keepdims=True)
        weights = jnp.exp(scores - largest)
        weight_sum = jnp.sum(weights, axis=1, keepdims=True)
        weights = weights.astype(BF16)

        def mix(i, mixed):
            for j in range(4):
                b = i * 4 + j
                got = jnp.dot(weights, cache_s[b, :, HD:], preferred_element_type=F32)
                mixed = jnp.where(wide_row == b, got, mixed)
            return mixed

        mixed = lax.fori_loop(0, 4, mix, jnp.zeros((4 * ROWS, HD), F32))
        if s == 0:
            n_copy(1 - half).wait_recv()
        new_key = jnp.concatenate([nkv_s[0].astype(F32)] * 4, axis=0)
        new_value = jnp.concatenate([nkv_s[1].astype(F32)] * 4, axis=0)
        own = jnp.sum(queries.astype(F32) * new_key, axis=1, keepdims=True) * scale
        top = jnp.maximum(largest, own)
        fade = jnp.exp(largest - top)
        own_weight = jnp.exp(own - top)
        attended = (mixed * fade + own_weight * new_value) / (weight_sum * fade + own_weight)
        at_s[s, :, 2] = attended.astype(BF16).reshape(4, ROWS, HD)
        for g in FAR_ORDER:
            a_copy(s, g).start()

    l_wo.wait()
    rdma(wout, wo_s.at[1 - k], w_ss.at[1], w_rs.at[1], sibling).wait_recv()

    def heads(s):
        for g in others:
            a_copy(s, (12 - g) % DP).wait_recv()
        return jnp.concatenate(
            [at_s[s, h].reshape(DP * ROWS, HD) for h in range(4)], axis=1
        )

    lhs0 = heads(0)

    def first(i, carry):
        cols = pl.ds(pl.multiple_of(i * 256, 256), 256)
        acc_s[:, cols] = jnp.dot(lhs0, wo_s[0, :, cols], preferred_element_type=F32)
        return carry

    lax.fori_loop(0, 8, first, 0)
    lhs1 = heads(1)

    def o_copy(to, slot):
        return rdma(po_s.at[to], ro_s.at[slot], o_ss.at[to], o_rs.at[slot], (d, to * 2 + k))

    def second(i, carry):
        p = (c // 2 + 1 + i) % 8
        cols = pl.ds(pl.multiple_of(p * 256, 256), 256)
        got = acc_s[:, cols] + jnp.dot(lhs1, wo_s[1, :, cols], preferred_element_type=F32)
        got = got.astype(BF16)
        for j in range(2):
            to = p * 2 + j
            po_s[to] = got[:, j * 128 : (j + 1) * 128].reshape(DP, ROWS, 128)

            @pl.when(to != c)
            def _():
                o_copy(to, c).start()

        return carry

    lax.fori_loop(0, 8, second, 0)

    total = po_s[c].astype(F32)
    for o in PLANE_ORDER[::-1]:
        src = chip(o)
        o_copy(src, src).wait_recv()
        total = total + ro_s[src].astype(F32)
    ps_s[...] = total.astype(BF16)

    def t_copy(g):
        return rdma(
            ps_s.at[g], r5_s.at[(12 - g) % DP], t_ss.at[g], t_rs.at[(12 - g) % DP], at_block(g)
        )

    for g in FAR_ORDER:
        t_copy(g).start()

    def finish(g, tile):
        cols = pl.ds(pl.multiple_of(block(g) * FEAT + c * 128, 128), 128)
        done = (hrow_s[:, cols].astype(F32) + tile.astype(F32)).astype(BF16)
        fin_s[g] = done
        g_s[g, :, lanes(c)] = done

    finish(2, ps_s[2])
    for g in others:
        t_copy((12 - g) % DP).wait_recv()
        finish(g, r5_s[g])

    def f_copy(o, src):
        return rdma(
            fin_s, g_s.at[:, :, lanes(src)], f_ss.at[o], f_rs.at[o], (d, chip(o) * 2 + k)
        )

    for o in PLANE_ORDER:
        f_copy(o, c).start()
    for o in PLANE_ORDER[::-1]:
        f_copy(o, back(o)).wait_recv()

    def e_copy(g, first_row):
        view = out.at[
            pl.ds(pl.multiple_of(first_row, ROWS), ROWS),
            pl.ds(pl.multiple_of(block(g) * FEAT, FEAT), FEAT),
        ]
        return (
            rdma(g_s.at[g], view, e_ss.at[g], e_rs.at[g], sibling),
            pltpu.make_async_copy(g_s.at[g], view, osem.at[g]),
        )

    for g in range(DP):
        there, local = e_copy(g, row0)
        there.start()
        local.start()

    for g in FAR_ORDER:
        x_copy(g).wait_send()
        kv_copy(g).wait_send()
        t_copy(g).wait_send()
        for s in range(2):
            q_copy(s, g).wait_send()
            a_copy(s, g).wait_send()
    for copy in w_copies:
        copy.wait_send()
    for o in PLANE_ORDER:
        xp_copy(o, c).wait_send()
        f_copy(o, c).wait_send()
        o_copy(chip(o), c).wait_send()
    n_copy(half).wait_send()
    for g in range(DP):
        there, local = e_copy(g, row0)
        there.wait_send()
        local.wait()
        e_copy(g, (1 - k) * ROWS)[0].wait_recv()


def body(hidden, gain, w_qkv, cache, lengths, w_out):
    any_space = pl.BlockSpec(memory_space=pl.ANY)
    vmem = pltpu.VMEM
    dma = pltpu.SemaphoreType.DMA
    scratch = [
        vmem((DP, ROWS, FEAT), BF16),
        vmem((3, ROWS, 128), BF16),
        vmem((3, ROWS, 128), BF16),
        vmem((1, FEAT), F32),
        vmem((2, FEAT, QW), BF16),
        vmem((FEAT, HD), BF16),
        vmem((2, QW, FEAT), BF16),
        vmem((ROWS, 256, 256), BF16),
        vmem((ROWS, DP * FEAT), BF16),
        vmem((2, DP, ROWS, QW), BF16),
        vmem((2, DP, ROWS, QW), BF16),
        vmem((DP, ROWS, HD), BF16),
        vmem((DP, ROWS, HD), BF16),
        vmem((2, ROWS, HD), BF16),
        vmem((2, 4, DP, ROWS, HD), BF16),
        vmem((DP * ROWS, FEAT), F32),
        vmem((CHIPS, DP, ROWS, 128), BF16),
        vmem((CHIPS, DP, ROWS, 128), BF16),
        vmem((DP, ROWS, 128), BF16),
        vmem((DP, ROWS, 128), BF16),
        vmem((DP, ROWS, 128), BF16),
        vmem((DP, ROWS, FEAT), BF16),
        dma((7,)),
        dma((2,)),
        dma((2,)),
        dma((DP,)),
        dma((DP,)),
        dma((CHIPS,)),
        dma((CHIPS,)),
        dma((DP,)),
        dma((DP,)),
        dma((2, DP)),
        dma((2, DP)),
        dma((1,)),
        dma((1,)),
        dma((2, DP)),
        dma((2, DP)),
        dma((CHIPS,)),
        dma((CHIPS,)),
        dma((DP,)),
        dma((DP,)),
        dma((CHIPS,)),
        dma((CHIPS,)),
        dma((DP,)),
        dma((DP,)),
        dma((DP,)),
    ]
    return pl.pallas_call(
        kernel,
        out_shape=jax.ShapeDtypeStruct(hidden.shape, hidden.dtype),
        in_specs=[
            any_space,
            any_space,
            any_space,
            any_space,
            pl.BlockSpec(memory_space=pltpu.SMEM),
            any_space,
        ],
        out_specs=any_space,
        scratch_shapes=scratch,
        compiler_params=pltpu.CompilerParams(
            collective_id=0, has_side_effects=True, vmem_limit_bytes=40 * 1024 * 1024
        ),
    )(hidden, gain.reshape(1, -1), w_qkv, cache, lengths, w_out)


def solution(mesh):
    return jax.shard_map(
        body,
        mesh=mesh,
        in_specs=(
            P("dp", None),
            P(),
            P("dp", "tensor"),
            P("dp", "tensor", None, None),
            P("dp"),
            P("tensor", "dp"),
        ),
        out_specs=P("dp", None),
        check_vma=False,
    )
```

time: 263 us -> 69 us (0.26)
  waiting for transfers between devices: 156 us -> 0 us
  blocking collectives: 76.2 us -> 0 us
  Pallas kernels: 0 us -> 59.4 us
  between operations: 13.5 us -> 0.02 us
  other arithmetic: 8.25 us -> 0 us
  local copies, waits for them, and re-layouts: 2 us -> 9.36 us
  matrix products: 7.18 us -> 0 us
    psum x1 -> x0, waiting for transfers between devices: 124 us -> none  [body(): lax.psum(partial_value.astype(jnp.bfloat16), 'tensor').astype(jnp.float32)]
    pallas_call x0 -> x1, Pallas kernels: none -> 59.4 us  [body(): pl.pallas_call(kernel, out_shape=jax.ShapeDtypeStruct(hidden.shape, hidde...]
    all_to_all x2 -> x0, blocking collectives: 57.4 us -> none  [the longest x1 36 us: body(): lax.all_to_all(normed, 'dp', split_axis=1, concat_axis=0, tiled=True)]
    reduce_scatter x1 -> x0, waiting for transfers between devices: 31.6 us -> none  [body(): lax.psum_scatter(jnp.dot(columns, w_qkv, preferred_element_type=jnp.float...]
    all_gather x1 -> x0, blocking collectives: 18.9 us -> none  [body(): lax.all_gather(attended, 'dp', axis=0, tiled=True)]
    unnamed x7 -> x13, local copies, waits for them, and re-layouts: 0.02 us -> 9.36 us
    dot_general x5 -> x0, matrix products: 7.18 us -> none  [the longest x1 2.37 us: attend(): jnp.einsum('rhd,rcd->rhc', queries, keys, preferred_element_type=jnp.floa...]
    convert_element_type x5 -> x0, other arithmetic: 5.15 us -> none  [the longest x1 2.75 us: body(): result = (wide + summed).astype(jnp.bfloat16)]
  transfers between devices with their start and end apart: 2 -> 0, of which waited for: 2 -> 0; matrix products, arithmetic and copies ran while one was open for 0% -> 0% of each run, Pallas kernels for 0% -> 0%
where the time goes in v1:
time: 69 us; the launch traced here: 68.7 us
  Pallas kernels  59.4 us (86%)
  local copies, waits for them, and re-layouts  9.36 us (14%)
    pallas_call x1, Pallas kernels, body(): pl.pallas_call(kernel, out_shape=jax.ShapeDtypeStruct(hidden.shape, hidde...  59.4 us
    unnamed x13, local copies, waits for them, and re-layouts  9.36 us

profile of v1, /device:TPU:1, one launch (start us, length us, event | category | flops | bytes accessed | tf_op | source)
XLA Modules:
  0.0 68.7 jit_solution(6391137634171204144)
XLA Ops:
  0.0 0.0 copy-start
  0.0 2.2 %copy-done = bf16[32,1,256,256]{3,2,1,0:T(8,128)(2,1)S(1)} copy-done((bf16[32,1,256,256]{3,2,1,0:T(8,128)(2,1)S(1)}, bf16[32,1,256,256]{3,2,1,0:T(8,128)(2,1)}, u32[]{:S(2)}) %copy-start) | copy-done | bytes 4194328
  2.2 0.0 copy-start.1
  2.2 1.9 %copy-done.1 = bf16[2048,768]{1,0:T(8,128)(2,1)S(1)} copy-done((bf16[2048,768]{1,0:T(8,128)(2,1)S(1)}, bf16[2048,768]{1,0:T(8,128)(2,1)}, u32[]{:S(2)}) %copy-start.1) | copy-done | bytes 3145752
  4.1 0.0 copy-start.2
  4.1 1.6 %copy-done.2 = bf16[512,2048]{1,0:T(8,128)(2,1)S(1)} copy-done((bf16[512,2048]{1,0:T(8,128)(2,1)S(1)}, bf16[512,2048]{1,0:T(8,128)(2,1)}, u32[]{:S(2)}) %copy-start.2) | copy-done | bytes 2097176
  5.7 0.0 copy-start.3
  5.7 1.2 %copy-done.3 = bf16[32,16384]{1,0:T(8,128)(2,1)S(1)} copy-done((bf16[32,16384]{1,0:T(8,128)(2,1)S(1)}, bf16[32,16384]{1,0:T(8,128)(2,1)}, u32[]{:S(2)}) %copy-start.3) | copy-done | bytes 1048600
  6.9 0.0 copy-start.4
  6.9 0.8 %copy-done.4 = f32[16384]{0:T(1024)S(1)} copy-done((f32[16384]{0:T(1024)S(1)}, f32[16384]{0:T(1024)}, u32[]{:S(2)}) %copy-start.4) | copy-done | bytes 65560
  7.7 0.0 copy-start.5
  7.7 0.7 copy-done.5
  8.4 59.4 %shard_map.64 = bf16[32,16384]{1,0:T(8,128)(2,1)S(1)} custom-call(bf16[32,16384]{1,0:T(8,128)(2,1)S(1)} %copy-done.3, f32[1,16384]{1,0:T(1,128)S(1)} %bitcast.1, bf16[2048,768]{1,0:T(8,128)(2,1)S(1)} %copy-done.1, bf16[32,1,256,256]{3,2,1,0:T(8,128)(2,1)S(1)} %copy-done, s32[32]{0:T(128)S(1)} %copy-done.5, bf16[512,2048]{1,0:T(8,128)(2,1)S(1)} %copy-done.2), custom_call_target="tpu_custom_call" | custom-call | tf_op jit(solution)/shard_map/pallas_call | solution.py:505
  67.8 1.0 %copy.8 = bf16[32,16384]{1,0:T(8,128)(2,1)} copy(bf16[32,16384]{1,0:T(8,128)(2,1)S(1)} %shard_map.64) | data formatting | bytes 2097152
Async XLA Ops:
  0.0 2.2 %copy-start = (bf16[32,1,256,256]{3,2,1,0:T(8,128)(2,1)S(1)}, bf16[32,1,256,256]{3,2,1,0:T(8,128)(2,1)}, u32[]{:S(2)}) copy-start(bf16[32,1,256,256]{3,2,1,0:T(8,128)(2,1)} %cache.1) | copy-start | bytes 12582916
  2.2 1.9 %copy-start.1 = (bf16[2048,768]{1,0:T(8,128)(2,1)S(1)}, bf16[2048,768]{1,0:T(8,128)(2,1)}, u32[]{:S(2)}) copy-start(bf16[2048,768]{1,0:T(8,128)(2,1)} %wqkv.1) | copy-start | bytes 9437188
  4.1 1.6 %copy-start.2 = (bf16[512,2048]{1,0:T(8,128)(2,1)S(1)}, bf16[512,2048]{1,0:T(8,128)(2,1)}, u32[]{:S(2)}) copy-start(bf16[512,2048]{1,0:T(8,128)(2,1)} %wout.1) | copy-start | bytes 6291460
  5.7 1.2 %copy-start.3 = (bf16[32,16384]{1,0:T(8,128)(2,1)S(1)}, bf16[32,16384]{1,0:T(8,128)(2,1)}, u32[]{:S(2)}) copy-start(bf16[32,16384]{1,0:T(8,128)(2,1)} %hid.1) | copy-start | bytes 3145732
  6.9 0.8 %copy-start.4 = (f32[16384]{0:T(1024)S(1)}, f32[16384]{0:T(1024)}, u32[]{:S(2)}) copy-start(f32[16384]{0:T(1024)} %param.7) | copy-start | bytes 196612
  7.7 0.7 copy-start.5

commit v2 on v1

v2 whole, which is shorter than its diff:
```python
import functools
import math

import jax
import jax.numpy as jnp
from jax import lax
from jax.experimental import pallas as pl
from jax.experimental.pallas import tpu as pltpu
from jax.sharding import PartitionSpec as P

DP = 8
CHIPS = 16
ROWS = 16
FEAT = 2048
HD = 128
QW = 512
NEAR = 5
ROPE_BASE = 500000.0
MESH = pl.DeviceIdType.MESH
F32 = jnp.float32
BF16 = jnp.bfloat16
REL = (7, 0, 1, 2, 6, 3, 4, 5)
MIRROR = (2, 1, 0, 4, 3, 7, 6, 5)
OWN = 1
FAR_ORDER = (6, 5, 7, 3, 4, 0, 2)
NEAR_ORDER = FAR_ORDER[::-1]
PLANE_ORDER = (10, 6, 14, 9, 11, 2, 8, 5, 7, 13, 15, 1, 3, 4, 12)


def kernel(
    hid,
    gain,
    wqkv,
    cache,
    lens,
    wout,
    out,
    raw_s,
    x_s,
    far_out,
    gain_s,
    wq_s,
    wkv_s,
    wo_s,
    cache_s,
    hrow_s,
    pq_s,
    rq_s,
    pkv_s,
    rkv_s,
    nkv_s,
    at_s,
    acc_s,
    po_s,
    ro_s,
    ps_s,
    fin_s,
    lsem,
    w_ss,
    w_rs,
    x_ss,
    x_rs,
    xp_ss,
    xp_rs,
    kv_ss,
    kv_rs,
    q_ss,
    q_rs,
    n_ss,
    n_rs,
    a_ss,
    a_rs,
    o_ss,
    o_rs,
    t_ss,
    t_rs,
    f_ss,
    f_rs,
    e_ss,
    e_rs,
):
    d = lax.axis_index("dp")
    t = lax.axis_index("tensor")
    k = t % 2
    c = t // 2
    cx = c // 4
    cy = c % 4
    half = c % 2
    row0 = pl.multiple_of(k * ROWS, ROWS)
    sibling = (d, c * 2 + (1 - k))
    sent = []

    def go(copy):
        copy.start()
        sent.append(copy)

    def block(g):
        return (d + REL[g]) % DP

    def at_block(g):
        return (block(g), t)

    def chip(o):
        px = (cx + o // 4) % 4
        py = (cy + o % 4) % 4
        return px * 4 + py

    def back(o):
        px = (cx + 4 - o // 4) % 4
        py = (cy + 4 - o % 4) % 4
        return px * 4 + py

    def rdma(src, dst, ss, rs, dev):
        return pltpu.make_async_remote_copy(
            src_ref=src, dst_ref=dst, send_sem=ss, recv_sem=rs, device_id=dev, device_id_type=MESH
        )

    def lanes(index):
        return pl.ds(pl.multiple_of(index * 128, 128), 128)

    def features(index):
        return pl.ds(pl.multiple_of(index * FEAT, FEAT), FEAT)

    l_gain = pltpu.make_async_copy(gain.at[:, features(d)], gain_s, lsem.at[1])
    l_x = pltpu.make_async_copy(hid.at[pl.ds(row0, ROWS), features(d)], raw_s.at[OWN], lsem.at[0])
    l_h = pltpu.make_async_copy(hid.at[pl.ds(row0, ROWS), :], hrow_s, lsem.at[2])
    l_wq = pltpu.make_async_copy(wqkv.at[:, pl.ds(0, QW)], wq_s.at[k], lsem.at[3])
    l_wkv = pltpu.make_async_copy(wqkv.at[:, lanes(4 + half)], wkv_s, lsem.at[4])
    l_cache = pltpu.make_async_copy(cache.at[pl.ds(row0, ROWS), 0], cache_s, lsem.at[5])
    l_wo = pltpu.make_async_copy(wout, wo_s.at[k], lsem.at[6])
    for copy in (l_gain, l_x, l_h, l_wkv, l_wq, l_cache, l_wo):
        copy.start()

    barrier = pltpu.get_barrier_semaphore()
    partners = [at_block(g) for g in FAR_ORDER]
    partners += [(d, chip(o) * 2 + k) for o in PLANE_ORDER]
    partners += [sibling]
    for dev in partners:
        pl.semaphore_signal(barrier, inc=1, device_id=dev, device_id_type=MESH)
    pl.semaphore_wait(barrier, len(partners))

    def x_copy(g):
        to = block(MIRROR[g])
        rows = pl.ds(row0, ROWS)
        if g < NEAR:
            return rdma(
                hid.at[rows, features(to)], raw_s.at[g], x_ss.at[g], x_rs.at[g], (to, t)
            )
        return rdma(
            hid.at[rows, lanes(to * (FEAT // 128) + c)],
            raw_s.at[g, :, lanes(c)],
            x_ss.at[g],
            x_rs.at[g],
            (to, t),
        )

    for g in FAR_ORDER:
        go(x_copy(g))
    go(rdma(wqkv.at[:, pl.ds(0, QW)], wq_s.at[k], w_ss.at[0], w_rs.at[0], sibling))
    go(rdma(wout, wo_s.at[k], w_ss.at[1], w_rs.at[1], sibling))

    l_h.wait()

    def square(i, total):
        cols = pl.ds(pl.multiple_of(i * 1024, 1024), 1024)
        part = hrow_s[:, cols].astype(F32)
        part = part * part
        for j in range(8):
            total = total + part[:, j * 128 : (j + 1) * 128]
        return total

    squares = lax.fori_loop(0, 16, square, jnp.zeros((ROWS, 128), F32))
    row_scale = lax.rsqrt(jnp.sum(squares, axis=1, keepdims=True) * (1.0 / (DP * FEAT)) + 1e-05)

    row_id = lax.broadcasted_iota(jnp.int32, (ROWS, HD), 0)
    lane_id = lax.broadcasted_iota(jnp.int32, (ROWS, HD), 1)
    length = jnp.zeros((ROWS, HD), jnp.int32)
    for b in range(ROWS):
        length = jnp.where(row_id == b, lens[k * ROWS + b], length)
    pair = jnp.where(lane_id < HD // 2, lane_id, lane_id - HD // 2).astype(F32)
    angle = length.astype(F32) * jnp.exp(pair * (-2.0 * math.log(ROPE_BASE) / HD))
    cosine = jnp.cos(angle)
    sine = jnp.sin(angle)
    sine = jnp.where(lane_id < HD // 2, -sine, sine)

    def rotate(v):
        return v * cosine + pltpu.roll(v, HD // 2, 1) * sine

    l_gain.wait()
    l_x.wait()

    def apply_gain(g):
        x_s[g] = (raw_s[g].astype(F32) * gain_s[...]).astype(BF16)

    apply_gain(OWN)

    for g in (5, 7, 6):
        x_copy(g).wait_recv()
    far = pl.ds(NEAR, DP - NEAR)
    tiles = raw_s[far, :, lanes(c)].astype(F32) * gain_s[:, lanes(c)].reshape(1, 1, 128)
    far_out[...] = tiles.astype(BF16)
    x_s[far, :, lanes(c)] = tiles.astype(BF16)

    def xp_copy(o, src):
        return rdma(
            far_out, x_s.at[far, :, lanes(src)], xp_ss.at[o], xp_rs.at[o], (d, chip(o) * 2 + k)
        )

    for o in PLANE_ORDER:
        go(xp_copy(o, c))

    for g in (0, 2, 3, 4):
        x_copy(g).wait_recv()
        apply_gain(g)

    def kv_copy(g):
        m = MIRROR[g]
        return rdma(pkv_s.at[g], rkv_s.at[m], kv_ss.at[g], kv_rs.at[m], at_block(g))

    def q_copy(s, g):
        m = MIRROR[g]
        return rdma(pq_s.at[s, g], rq_s.at[s, m], q_ss.at[s, g], q_rs.at[s, m], at_block(g))

    def project(lo, n, order):
        lhs = x_s[pl.ds(lo, n)].reshape(n * ROWS, FEAT)
        got = jnp.dot(lhs, wkv_s[...], preferred_element_type=F32)
        pkv_s[pl.ds(lo, n)] = got.astype(BF16).reshape(n, ROWS, HD)
        for g in order:
            go(kv_copy(g))
        for s in range(2):
            for j in range(2):
                cols = slice(j * 256, (j + 1) * 256)
                got = jnp.dot(lhs, wq_s[s, :, cols], preferred_element_type=F32)
                pq_s[s, pl.ds(lo, n), :, cols] = got.astype(BF16).reshape(n, ROWS, 256)
            for g in order:
                go(q_copy(s, g))

    l_wkv.wait()
    l_wq.wait()
    rdma(
        wqkv.at[:, pl.ds(0, QW)], wq_s.at[1 - k], w_ss.at[0], w_rs.at[0], sibling
    ).wait_recv()

    project(0, NEAR, (3, 4, 0, 2))

    for o in PLANE_ORDER[::-1]:
        xp_copy(o, back(o)).wait_recv()

    project(NEAR, DP - NEAR, (6, 5, 7))

    total = pkv_s[OWN].astype(F32)
    for g in NEAR_ORDER:
        kv_copy(MIRROR[g]).wait_recv()
        total = total + rkv_s[g].astype(F32)
    total = total * row_scale
    nkv_s[half] = jnp.where(half == 0, rotate(total), total).astype(BF16)
    beside = c + 1 - 2 * half

    def n_copy(which):
        return rdma(
            nkv_s.at[which], nkv_s.at[which], n_ss.at[0], n_rs.at[0], (d, beside * 2 + k)
        )

    go(n_copy(half))

    l_cache.wait()
    wide_row = lax.broadcasted_iota(jnp.int32, (4 * ROWS, HD), 0) % ROWS
    wide_lane = lax.broadcasted_iota(jnp.int32, (256, 4 * ROWS), 1) % ROWS
    position = lax.broadcasted_iota(jnp.int32, (4 * ROWS, 256), 1)
    limit = jnp.concatenate([length[:, :1]] * 4, axis=0)
    scale = 1.0 / HD**0.5

    def a_copy(s, g):
        m = MIRROR[g]
        return rdma(
            at_s.at[s, :, OWN], at_s.at[s, :, m], a_ss.at[s, g], a_rs.at[s, m], at_block(g)
        )

    for s in range(2):
        total = pq_s[s, OWN].astype(F32)
        for g in NEAR_ORDER:
            q_copy(s, MIRROR[g]).wait_recv()
            total = total + rq_s[s, g].astype(F32)
        total = total * row_scale

        queries = jnp.concatenate(
            [rotate(total[:, h * HD : (h + 1) * HD]) for h in range(4)], axis=0
        ).astype(BF16)
        turned = queries.astype(F32).T.astype(BF16)

        def score(i, scores):
            for j in range(4):
                b = i * 4 + j
                got = jnp.dot(cache_s[b, :, :HD], turned, preferred_element_type=F32)
                scores = jnp.where(wide_lane == b, got, scores)
            return scores

        scores = lax.fori_loop(0, 4, score, jnp.zeros((256, 4 * ROWS), F32))
        scores = jnp.where(position < limit, scores.T * scale, -jnp.inf)
        largest = jnp.max(scores, axis=1, keepdims=True)
        weights = jnp.exp(scores - largest)
        weight_sum = jnp.sum(weights, axis=1, keepdims=True)
        weights = weights.astype(BF16)

        def mix(i, mixed):
            for j in range(4):
                b = i * 4 + j
                got = jnp.dot(weights, cache_s[b, :, HD:], preferred_element_type=F32)
                mixed = jnp.where(wide_row == b, got, mixed)
            return mixed

        mixed = lax.fori_loop(0, 4, mix, jnp.zeros((4 * ROWS, HD), F32))
        if s == 0:
            n_copy(1 - half).wait_recv()
        new_key = jnp.concatenate([nkv_s[0].astype(F32)] * 4, axis=0)
        new_value = jnp.concatenate([nkv_s[1].astype(F32)] * 4, axis=0)
        own = jnp.sum(queries.astype(F32) * new_key, axis=1, keepdims=True) * scale
        top = jnp.maximum(largest, own)
        fade = jnp.exp(largest - top)
        own_weight = jnp.exp(own - top)
        attended = (mixed * fade + own_weight * new_value) / (weight_sum * fade + own_weight)
        at_s[s, :, OWN] = attended.astype(BF16).reshape(4, ROWS, HD)
        for g in FAR_ORDER:
            go(a_copy(s, g))

    l_wo.wait()
    rdma(wout, wo_s.at[1 - k], w_ss.at[1], w_rs.at[1], sibling).wait_recv()

    def heads(s):
        for g in NEAR_ORDER:
            a_copy(s, MIRROR[g]).wait_recv()
        return jnp.concatenate([at_s[s, h].reshape(DP * ROWS, HD) for h in range(4)], axis=1)

    def o_copy(to, slot):
        return rdma(po_s.at[to], ro_s.at[slot], o_ss.at[to], o_rs.at[slot], (d, to * 2 + k))

    lhs0 = heads(0)

    def first_half(i, carry):
        cols = pl.ds(pl.multiple_of(i * 256, 256), 256)
        acc_s[:, cols] = jnp.dot(lhs0, wo_s[0, :, cols], preferred_element_type=F32)
        return carry

    lax.fori_loop(0, 8, first_half, 0)
    lhs1 = heads(1)

    def second_half(i, carry):
        p = (cx + 2 + i // 2) % 4 * 2 + (cy // 2 + 1 + i) % 2
        cols = pl.ds(pl.multiple_of(p * 256, 256), 256)
        got = acc_s[:, cols] + jnp.dot(lhs1, wo_s[1, :, cols], preferred_element_type=F32)
        got = got.astype(BF16)
        for j in range(2):
            to = p * 2 + j
            po_s[to] = got[:, j * 128 : (j + 1) * 128].reshape(DP, ROWS, 128)

            @pl.when(to != c)
            def _():
                o_copy(to, c).start()

        return carry

    lax.fori_loop(0, 8, second_half, 0)
    for o in PLANE_ORDER:
        sent.append(o_copy(chip(o), c))

    total = po_s[c].astype(F32)
    for o in PLANE_ORDER[::-1]:
        src = back(o)
        o_copy(src, src).wait_recv()
        total = total + ro_s[src].astype(F32)
    ps_s[...] = (raw_s[:, :, lanes(c)].astype(F32) + total).astype(BF16)

    def t_copy(g):
        return rdma(ps_s.at[g], fin_s.at[d], t_ss.at[g], t_rs.at[MIRROR[g]], at_block(g))

    for g in FAR_ORDER:
        go(t_copy(g))
    fin_s[d] = ps_s[OWN]
    for g in NEAR_ORDER:
        rdma(
            ps_s.at[g], fin_s.at[block(g)], t_ss.at[g], t_rs.at[g], at_block(g)
        ).wait_recv()

    def f_copy(o, src):
        return rdma(
            fin_s, out.at[k, :, :, lanes(src)], f_ss.at[o], f_rs.at[o], (d, chip(o) * 2 + k)
        )

    def e_copy(o, src, half_of):
        view = out.at[half_of, :, :, lanes(src)]
        return rdma(view, view, e_ss.at[o], e_rs.at[o], sibling)

    for o in PLANE_ORDER:
        go(f_copy(o, c))
    out[k, :, :, lanes(c)] = fin_s[...]
    go(e_copy(0, c, k))
    for o in PLANE_ORDER[::-1]:
        f_copy(o, back(o)).wait_recv()
        go(e_copy(o, back(o), k))

    e_copy(0, c, 1 - k).wait_recv()
    for o in PLANE_ORDER[::-1]:
        e_copy(o, back(o), 1 - k).wait_recv()

    for copy in sent:
        copy.wait_send()


def body(hidden, gain, w_qkv, cache, lengths, w_out):
    any_space = pl.BlockSpec(memory_space=pl.ANY)
    vmem = pltpu.VMEM
    dma = pltpu.SemaphoreType.DMA
    scratch = [
        vmem((DP, ROWS, FEAT), BF16),
        vmem((DP, ROWS, FEAT), BF16),
        vmem((DP - NEAR, ROWS, 128), BF16),
        vmem((1, FEAT), F32),
        vmem((2, FEAT, QW), BF16),
        vmem((FEAT, HD), BF16),
        vmem((2, QW, FEAT), BF16),
        vmem((ROWS, 256, 256), BF16),
        vmem((ROWS, DP * FEAT), BF16),
        vmem((2, DP, ROWS, QW), BF16),
        vmem((2, DP, ROWS, QW), BF16),
        vmem((DP, ROWS, HD), BF16),
        vmem((DP, ROWS, HD), BF16),
        vmem((2, ROWS, HD), BF16),
        vmem((2, 4, DP, ROWS, HD), BF16),
        vmem((DP * ROWS, FEAT), F32),
        vmem((CHIPS, DP, ROWS, 128), BF16),
        vmem((CHIPS, DP, ROWS, 128), BF16),
        vmem((DP, ROWS, 128), BF16),
        vmem((DP, ROWS, 128), BF16),
        dma((7,)),
        dma((2,)),
        dma((2,)),
        dma((DP,)),
        dma((DP,)),
        dma((CHIPS,)),
        dma((CHIPS,)),
        dma((DP,)),
        dma((DP,)),
        dma((2, DP)),
        dma((2, DP)),
        dma((1,)),
        dma((1,)),
        dma((2, DP)),
        dma((2, DP)),
        dma((CHIPS,)),
        dma((CHIPS,)),
        dma((DP,)),
        dma((DP,)),
        dma((CHIPS,)),
        dma((CHIPS,)),
        dma((CHIPS,)),
        dma((CHIPS,)),
    ]
    halves = pl.pallas_call(
        kernel,
        out_shape=vmem((2, DP, ROWS, FEAT), BF16),
        in_specs=[
            any_space,
            any_space,
            any_space,
            any_space,
            pl.BlockSpec(memory_space=pltpu.SMEM),
            any_space,
        ],
        out_specs=pl.BlockSpec(memory_space=vmem),
        scratch_shapes=scratch,
        compiler_params=pltpu.CompilerParams(
            collective_id=0, has_side_effects=True, vmem_limit_bytes=60 * 1024 * 1024
        ),
    )(hidden, gain.reshape(1, -1), w_qkv, cache, lengths, w_out)
    tiles = halves.reshape(2, DP, 2, 8, FEAT).transpose(0, 2, 3, 1, 4)
    return tiles.reshape(hidden.shape)


def solution(mesh):
    return jax.shard_map(
        body,
        mesh=mesh,
        in_specs=(
            P("dp", None),
            P(),
            P("dp", "tensor"),
            P("dp", "tensor", None, None),
            P("dp"),
            P("tensor", "dp"),
        ),
        out_specs=P("dp", None),
        check_vma=False,
    )
```

time: 69 us -> 59.8 us (0.87)
  local copies, waits for them, and re-layouts: 9.36 us -> 1.08 us
  Pallas kernels: 59.4 us -> 58.6 us
    unnamed x13 -> x0, local copies, waits for them, and re-layouts: 9.36 us -> none
    transpose x0 -> x1, local copies, waits for them, and re-layouts: none -> 1.08 us  [body(): tiles = halves.reshape(2, DP, 2, 8, FEAT).transpose(0, 2, 3, 1, 4)]
    pallas_call x1, Pallas kernels: 59.4 us -> 58.6 us  [body(): pl.pallas_call(kernel, out_shape=vmem((2, DP, ROWS, FEAT), BF16), in_spec...]
where the time goes in v2:
time: 59.8 us; the launch traced here: 59.7 us
  Pallas kernels  58.6 us (98%)
  local copies, waits for them, and re-layouts  1.08 us (2%)
    pallas_call x1, Pallas kernels, body(): pl.pallas_call(kernel, out_shape=vmem((2, DP, ROWS, FEAT), BF16), in_spec...  58.6 us

profile of v2, /device:TPU:1, one launch (start us, length us, event | category | flops | bytes accessed | tf_op | source)
XLA Modules:
  0.0 59.7 jit_solution(5501011756353490478)
XLA Ops:
  0.0 58.6 %shard_map.64 = bf16[2,8,16,2048]{3,2,1,0:T(8,128)(2,1)S(1)} custom-call(bf16[32,16384]{1,0:T(8,128)(2,1)} %hid.1, f32[1,16384]{1,0:T(1,128)} %bitcast.6, bf16[2048,768]{1,0:T(8,128)(2,1)} %wqkv.1, bf16[32,1,256,256]{3,2,1,0:T(8,128)(2,1)} %cache.1, s32[32]{0:T(128)} %lens.1, bf16[512,2048]{1,0:T(8,128)(2,1)} %wout.1), custom_call_target="tpu_custom_call" | custom-call | tf_op jit(solution)/shard_map/pallas_call | solution.py:458
  58.6 1.1 %copy.7 = bf16[2,2,8,8,2048]{4,2,3,1,0:T(8,128)(2,1)} copy(bf16[2,2,8,8,2048]{4,2,1,3,0:T(8,128)(2,1)S(1)} %bitcast.5) | data formatting | bytes 2097152 | tf_op jit(solution)/shard_map/transpose | solution.py:475

commit v3 on v2

--- a/solution.py
+++ b/solution.py
@@ -14,7 +14,7 @@
 FEAT = 2048
 HD = 128
 QW = 512
-NEAR = 5
+NEAR = 3
 ROPE_BASE = 500000.0
 MESH = pl.DeviceIdType.MESH
 F32 = jnp.float32
@@ -22,6 +22,7 @@
 REL = (7, 0, 1, 2, 6, 3, 4, 5)
 MIRROR = (2, 1, 0, 4, 3, 7, 6, 5)
 OWN = 1
+PARTS = ((1, 0, 2, 3, 4), (5, 7, 6))
 FAR_ORDER = (6, 5, 7, 3, 4, 0, 2)
 NEAR_ORDER = FAR_ORDER[::-1]
 PLANE_ORDER = (10, 6, 14, 9, 11, 2, 8, 5, 7, 13, 15, 1, 3, 4, 12)
@@ -194,7 +195,7 @@
 
     apply_gain(OWN)
 
-    for g in (5, 7, 6):
+    for g in (3, 4, 5, 7, 6):
         x_copy(g).wait_recv()
     far = pl.ds(NEAR, DP - NEAR)
     tiles = raw_s[far, :, lanes(c)].astype(F32) * gain_s[:, lanes(c)].reshape(1, 1, 128)
@@ -209,7 +210,7 @@
     for o in PLANE_ORDER:
         go(xp_copy(o, c))
 
-    for g in (0, 2, 3, 4):
+    for g in (0, 2):
         x_copy(g).wait_recv()
         apply_gain(g)
 
@@ -241,12 +242,12 @@
         wqkv.at[:, pl.ds(0, QW)], wq_s.at[1 - k], w_ss.at[0], w_rs.at[0], sibling
     ).wait_recv()
 
-    project(0, NEAR, (3, 4, 0, 2))
+    project(0, NEAR, (0, 2))
 
     for o in PLANE_ORDER[::-1]:
         xp_copy(o, back(o)).wait_recv()
 
-    project(NEAR, DP - NEAR, (6, 5, 7))
+    project(NEAR, DP - NEAR, (6, 5, 7, 3, 4))
 
     total = pkv_s[OWN].astype(F32)
     for g in NEAR_ORDER:
@@ -376,26 +377,39 @@
     for g in FAR_ORDER:
         go(t_copy(g))
     fin_s[d] = ps_s[OWN]
-    for g in NEAR_ORDER:
-        rdma(
-            ps_s.at[g], fin_s.at[block(g)], t_ss.at[g], t_rs.at[g], at_block(g)
-        ).wait_recv()
-
-    def f_copy(o, src):
+
+    def f_copy(q, o, src, which):
         return rdma(
-            fin_s, out.at[k, :, :, lanes(src)], f_ss.at[o], f_rs.at[o], (d, chip(o) * 2 + k)
+            fin_s.at[which],
+            out.at[k, which, :, lanes(src)],
+            f_ss.at[q, o],
+            f_rs.at[q, o],
+            (d, chip(o) * 2 + k),
         )
+
+    def f_all(q, o, src):
+        return f_copy(q, o, src, pl.ds(0, len(PARTS[q])))
+
+    for q, part in enumerate(PARTS):
+        for g in part:
+            if g != OWN:
+                rdma(
+                    ps_s.at[g], fin_s.at[block(g)], t_ss.at[g], t_rs.at[g], at_block(g)
+                ).wait_recv()
+        for o in PLANE_ORDER:
+            for g in part:
+                f_copy(q, o, c, block(g)).start()
+            sent.append(f_all(q, o, c))
 
     def e_copy(o, src, half_of):
         view = out.at[half_of, :, :, lanes(src)]
         return rdma(view, view, e_ss.at[o], e_rs.at[o], sibling)
 
-    for o in PLANE_ORDER:
-        go(f_copy(o, c))
     out[k, :, :, lanes(c)] = fin_s[...]
     go(e_copy(0, c, k))
     for o in PLANE_ORDER[::-1]:
-        f_copy(o, back(o)).wait_recv()
+        for q in range(len(PARTS)):
+            f_all(q, o, back(o)).wait_recv()
         go(e_copy(o, back(o), k))
 
     e_copy(0, c, 1 - k).wait_recv()
@@ -450,8 +464,8 @@
         dma((CHIPS,)),
         dma((DP,)),
         dma((DP,)),
-        dma((CHIPS,)),
-        dma((CHIPS,)),
+        dma((len(PARTS), CHIPS)),
+        dma((len(PARTS), CHIPS)),
         dma((CHIPS,)),
         dma((CHIPS,)),
     ]

time: 59.8 us -> 59.1 us (0.988)
  Pallas kernels: 58.6 us -> 58 us
    pallas_call x1, Pallas kernels: 58.6 us -> 58 us  [body(): pl.pallas_call(kernel, out_shape=vmem((2, DP, ROWS, FEAT), BF16), in_spec...]
where the time goes in v3:
time: 59.1 us
  Pallas kernels  58 us (98%)
  local copies, waits for them, and re-layouts  1.08 us (2%)
    pallas_call x1, Pallas kernels, body(): pl.pallas_call(kernel, out_shape=vmem((2, DP, ROWS, FEAT), BF16), in_spec...  58 us

profile of v3, /device:TPU:1, one launch (start us, length us, event | category | flops | bytes accessed | tf_op | source)
XLA Modules:
  0.0 59.1 jit_solution(8245186190471967992)
XLA Ops:
  0.0 58.0 %shard_map.64 = bf16[2,8,16,2048]{3,2,1,0:T(8,128)(2,1)S(1)} custom-call(bf16[32,16384]{1,0:T(8,128)(2,1)} %hid.1, f32[1,16384]{1,0:T(1,128)} %bitcast.6, bf16[2048,768]{1,0:T(8,128)(2,1)} %wqkv.1, bf16[32,1,256,256]{3,2,1,0:T(8,128)(2,1)} %cache.1, s32[32]{0:T(128)} %lens.1, bf16[512,2048]{1,0:T(8,128)(2,1)} %wout.1), custom_call_target="tpu_custom_call" | custom-call | tf_op jit(solution)/shard_map/pallas_call | solution.py:472
  58.0 1.1 %copy.7 = bf16[2,2,8,8,2048]{4,2,3,1,0:T(8,128)(2,1)} copy(bf16[2,2,8,8,2048]{4,2,1,3,0:T(8,128)(2,1)S(1)} %bitcast.5) | data formatting | bytes 2097152 | tf_op jit(solution)/shard_map/transpose | solution.py:489

commit v4 on v3

--- a/solution.py
+++ b/solution.py
@@ -22,7 +22,7 @@
 REL = (7, 0, 1, 2, 6, 3, 4, 5)
 MIRROR = (2, 1, 0, 4, 3, 7, 6, 5)
 OWN = 1
-PARTS = ((1, 0, 2, 3, 4), (5, 7, 6))
+PARTS = ((1, 0, 2), (3, 4, 5, 7, 6))
 FAR_ORDER = (6, 5, 7, 3, 4, 0, 2)
 NEAR_ORDER = FAR_ORDER[::-1]
 PLANE_ORDER = (10, 6, 14, 9, 11, 2, 8, 5, 7, 13, 15, 1, 3, 4, 12)

time: 59.1 us -> 58.9 us (level)
  no operation moved by 1% of the time
where the time goes in v4:
time: 58.9 us; the launch traced here: 58.8 us
  Pallas kernels  57.8 us (98%)
  local copies, waits for them, and re-layouts  1.08 us (2%)
    pallas_call x1, Pallas kernels, body(): pl.pallas_call(kernel, out_shape=vmem((2, DP, ROWS, FEAT), BF16), in_spec...  57.8 us

profile of v4, /device:TPU:1, one launch (start us, length us, event | category | flops | bytes accessed | tf_op | source)
XLA Modules:
  0.0 58.8 jit_solution(17856866322936971104)
XLA Ops:
  0.0 57.8 %shard_map.64 = bf16[2,8,16,2048]{3,2,1,0:T(8,128)(2,1)S(1)} custom-call(bf16[32,16384]{1,0:T(8,128)(2,1)} %hid.1, f32[1,16384]{1,0:T(1,128)} %bitcast.6, bf16[2048,768]{1,0:T(8,128)(2,1)} %wqkv.1, bf16[32,1,256,256]{3,2,1,0:T(8,128)(2,1)} %cache.1, s32[32]{0:T(128)} %lens.1, bf16[512,2048]{1,0:T(8,128)(2,1)} %wout.1), custom_call_target="tpu_custom_call" | custom-call | tf_op jit(solution)/shard_map/pallas_call | solution.py:472
  57.8 1.1 %copy.7 = bf16[2,2,8,8,2048]{4,2,3,1,0:T(8,128)(2,1)} copy(bf16[2,2,8,8,2048]{4,2,1,3,0:T(8,128)(2,1)S(1)} %bitcast.5) | data formatting | bytes 2097152 | tf_op jit(solution)/shard_map/transpose | solution.py:489

commit v5 on v4

--- a/solution.py
+++ b/solution.py
@@ -158,7 +158,6 @@
     for g in FAR_ORDER:
         go(x_copy(g))
     go(rdma(wqkv.at[:, pl.ds(0, QW)], wq_s.at[k], w_ss.at[0], w_rs.at[0], sibling))
-    go(rdma(wout, wo_s.at[k], w_ss.at[1], w_rs.at[1], sibling))
 
     l_h.wait()
 
@@ -236,6 +235,7 @@
             for g in order:
                 go(q_copy(s, g))
 
+    go(rdma(wout, wo_s.at[k], w_ss.at[1], w_rs.at[1], sibling))
     l_wkv.wait()
     l_wq.wait()
     rdma(
@@ -390,6 +390,8 @@
     def f_all(q, o, src):
         return f_copy(q, o, src, pl.ds(0, len(PARTS[q])))
 
+    earlier = list(sent)
+    sent.clear()
     for q, part in enumerate(PARTS):
         for g in part:
             if g != OWN:
@@ -407,6 +409,8 @@
 
     out[k, :, :, lanes(c)] = fin_s[...]
     go(e_copy(0, c, k))
+    for copy in earlier:
+        copy.wait_send()
     for o in PLANE_ORDER[::-1]:
         for q in range(len(PARTS)):
             f_all(q, o, back(o)).wait_recv()

time: 58.9 us -> 58.8 us (level)
  no operation moved by 1% of the time
where the time goes in v5:
time: 58.8 us; the launch traced here: 58.7 us
  Pallas kernels  57.6 us (98%)
  local copies, waits for them, and re-layouts  1.08 us (2%)
    pallas_call x1, Pallas kernels, body(): pl.pallas_call(kernel, out_shape=vmem((2, DP, ROWS, FEAT), BF16), in_spec...  57.6 us

profile of v5, /device:TPU:1, one launch (start us, length us, event | category | flops | bytes accessed | tf_op | source)
XLA Modules:
  0.0 58.7 jit_solution(1897501972270927433)
XLA Ops:
  0.0 57.6 %shard_map.64 = bf16[2,8,16,2048]{3,2,1,0:T(8,128)(2,1)S(1)} custom-call(bf16[32,16384]{1,0:T(8,128)(2,1)} %hid.1, f32[1,16384]{1,0:T(1,128)} %bitcast.6, bf16[2048,768]{1,0:T(8,128)(2,1)} %wqkv.1, bf16[32,1,256,256]{3,2,1,0:T(8,128)(2,1)} %cache.1, s32[32]{0:T(128)} %lens.1, bf16[512,2048]{1,0:T(8,128)(2,1)} %wout.1), custom_call_target="tpu_custom_call" | custom-call | tf_op jit(solution)/shard_map/pallas_call | solution.py:476
  57.6 1.1 %copy.7 = bf16[2,2,8,8,2048]{4,2,3,1,0:T(8,128)(2,1)} copy(bf16[2,2,8,8,2048]{4,2,1,3,0:T(8,128)(2,1)S(1)} %bitcast.5) | data formatting | bytes 2097152 | tf_op jit(solution)/shard_map/transpose | solution.py:493
